TPU v7x, 512 devices: a whole 4x8x8 slice. The times are simulated.
512 devices in a mesh: ctx: 128 (over z, y, core), head: 4 (over x).
Axes of the slice: x: 4, y: 8, z: 8, core: 2. Of those that a mesh axis runs over, the one named last changes fastest.
Arguments:
- features: bfloat16 [32768, 1024], P('ctx', 'head'), may hold values from -30 to 30
- w_qkv: bfloat16 [1024, 3, 1024], P(None, None, 'head'), may hold values from -1 to 1
- block_links: int32 [256, 9], P('ctx'), may hold values from -1 to 255, as said below
- d_out: bfloat16 [32768, 1024], P('ctx', 'head'), may hold values from -6 to 6
Outputs:
- attended: bfloat16 [32768, 1024], P('ctx', 'head')
- grad_features: bfloat16 [32768, 1024], P('ctx', 'head')
Inputs may be any that keep to these rules, and one draw needn't show every extreme that they name: `block_links`: row q lists in order the key blocks q - 1 to q + 1; then p - 1 to p + 1, p being the block on the previous coil turn; then n - 1 to n + 1, n being the block on the next coil turn. q - p and n - q lie between 3 and 5, and a distance of 5 occurs in both directions in every draw. A coil neighbour may be absent; the entries of an absent neighbour and entries outside the sequence are -1. Live entries of a row are distinct.
All inputs are finite; a program needn't handle non-finite values.
Results may differ from a plain program's by a relative error of at most 0.025.
Values may be sent and summed in bfloat16 or wider, within the bound.
A program may use at most 64 MiB of HBM per device.

v0:
```python
import jax
import jax.numpy as jnp
from jax import lax
from jax.sharding import PartitionSpec as P

HD = 128
BLK = 128
OMAX = 3


def shifted(value, axis, steps):
    count = lax.axis_size(axis)
    first, last = (max(0, -steps), min(count, count - steps))
    return lax.ppermute(value, axis, [(source, source + steps) for source in range(first, last)])


def rounded_terms(values):
    return lax.optimization_barrier(values.astype(jnp.bfloat16)).astype(jnp.float32)


def body(features, w_qkv, block_links, d_out):
    tok_rows = d_out.shape[0]
    local_width = w_qkv.shape[2]
    model_width = w_qkv.shape[0]
    resident_tiles = tok_rows // BLK
    heads_here = local_width // HD
    score_scale = HD ** (-0.5)
    w_flat = w_qkv.reshape(model_width, 3 * local_width)
    projected = jnp.dot(
        lax.all_gather(features, "head", axis=1, tiled=True),
        w_flat,
        preferred_element_type=jnp.float32,
    )
    projected = projected.astype(jnp.bfloat16)
    query_blocks = projected[:, :local_width].reshape(resident_tiles, BLK, heads_here, HD)
    pair_blocks = projected[:, local_width:].reshape(resident_tiles, BLK, 2 * local_width)
    lower_shards = []
    upper_shards = []
    for offset in range(1, OMAX + 1):
        for direction in (1, -1):
            arrived = shifted(pair_blocks, "ctx", direction * offset)
            if direction > 0:
                lower_shards.append(arrived)
            else:
                upper_shards.append(arrived)
    window_pairs = jnp.concatenate(
        list(reversed(lower_shards)) + [pair_blocks] + upper_shards, axis=0
    )
    extent = window_pairs.shape[0]
    own_start = OMAX * resident_tiles
    anchor = lax.axis_index("ctx") * resident_tiles - own_start
    live_slot = block_links >= 0
    slot_index = jnp.where(live_slot, block_links - anchor, own_start)
    drop_index = jnp.where(live_slot, block_links - anchor, extent)
    slots = block_links.shape[1]
    selected = window_pairs[slot_index].reshape(resident_tiles, slots * BLK, 2, heads_here, HD)
    lookup_rows = selected[:, :, 0]
    content_rows = selected[:, :, 1]
    key_mask = jnp.repeat(live_slot, BLK, axis=1)[:, None, None, :]
    grad_blocks = d_out.reshape(resident_tiles, BLK, heads_here, HD)
    scores = (
        jnp.einsum("iqhd,ikhd->ihqk", query_blocks, lookup_rows, preferred_element_type=jnp.float32)
        * score_scale
    )
    largest = jnp.max(jnp.where(key_mask, scores, -1e30), axis=-1, keepdims=True)
    exp_total = jnp.sum(jnp.where(key_mask, jnp.exp(scores - largest), 0.0), axis=-1, keepdims=True)
    normalized = jnp.where(key_mask, jnp.exp(scores - largest), 0.0) / exp_total
    softmax_share = normalized.astype(jnp.bfloat16)
    attended = jnp.einsum(
        "ihqk,ikhd->iqhd", softmax_share, content_rows, preferred_element_type=jnp.float32
    ).astype(jnp.bfloat16)
    row_dot = jnp.sum(grad_blocks.astype(jnp.float32) * attended.astype(jnp.float32), axis=-1)
    value_terms = jnp.einsum(
        "ihqk,iqhd->ikhd", softmax_share, grad_blocks, preferred_element_type=jnp.float32
    )
    probability_gradient = jnp.einsum(
        "iqhd,ikhd->ihqk", grad_blocks, content_rows, preferred_element_type=jnp.float32
    )
    recomputed = jnp.where(key_mask, jnp.exp(scores - largest), 0.0) / exp_total
    score_derivative = (
        recomputed * (probability_gradient - jnp.transpose(row_dot, (0, 2, 1))[:, :, :, None])
    ).astype(jnp.bfloat16)
    query_grad = (
        jnp.einsum(
            "ihqk,ikhd->iqhd", score_derivative, lookup_rows, preferred_element_type=jnp.float32
        )
        * score_scale
    )
    key_terms = (
        jnp.einsum(
            "ihqk,iqhd->ikhd", score_derivative, query_blocks, preferred_element_type=jnp.float32
        )
        * score_scale
    )
    flat_index = drop_index.reshape(-1)
    slot_owner = (flat_index[None, :] == jnp.arange(extent, dtype=jnp.int32)[:, None]).astype(
        jnp.float32
    )
    slot_terms = jnp.concatenate(
        [
            key_terms.reshape(resident_tiles * slots, BLK, local_width),
            value_terms.reshape(resident_tiles * slots, BLK, local_width),
        ],
        axis=2,
    )
    pair_grads = jnp.einsum(
        "es,sbc->ebc",
        slot_owner,
        slot_terms,
        precision=lax.Precision.HIGHEST,
        preferred_element_type=jnp.float32,
    )
    grad_total = rounded_terms(pair_grads[own_start : own_start + resident_tiles])
    for offset in range(1, OMAX + 1):
        for direction in (1, -1):
            domain_first_index = own_start + direction * offset * resident_tiles
            region = pair_grads[domain_first_index : domain_first_index + resident_tiles]
            arrived = shifted(region.astype(jnp.bfloat16), "ctx", direction * offset).astype(
                jnp.float32
            )
            grad_total = grad_total + arrived
    attended_all = attended.reshape(tok_rows, local_width)
    query_all = query_grad.reshape(tok_rows, local_width)
    grad_projected = jnp.concatenate(
        [query_all, grad_total.reshape(tok_rows, 2 * local_width)], axis=1
    ).astype(jnp.bfloat16)
    partial_sum = jnp.einsum(
        "tc,dc->td", grad_projected, w_flat, preferred_element_type=jnp.float32
    )
    grad_features = lax.psum_scatter(
        partial_sum.astype(jnp.bfloat16), "head", scatter_dimension=1, tiled=True
    )
    return (attended_all, grad_features)


def solution(mesh):
    return jax.shard_map(
        body,
        mesh=mesh,
        in_specs=(P("ctx", "head"), P(None, None, "head"), P("ctx", None), P("ctx", "head")),
        out_specs=(P("ctx", "head"), P("ctx", "head")),
        check_vma=False,
    )
```

profile of v0, /device:TPU:8, one launch (start us, length us, event | category | flops | bytes accessed | tf_op | source)
XLA Modules:
  0.0 183.2 jit_solution(3778253173048944143)
XLA Ops:
  7.2 13.3 %all_gather.3 = bf16[256,1024]{1,0:T(8,128)(2,1)S(1)} all-gather(bf16[256,256]{1,0:T(8,128)(2,1)} %param.4), channel_id=1, replica_groups=mesh['ctx'=128,'head'=4] {'head'}, dimensions={1}, use_global_device_ids=true | all-gather | bytes 655360 | tf_op jit(solution)/shard_map/all_gather | solution.py:30
  20.6 1.7 copy.33
  24.3 7.4 %collective-permute-start.4 = (bf16[2,128,512]{2,1,0:T(8,128)(2,1)S(1)}, bf16[2,128,512]{2,1,0:T(8,128)(2,1)S(1)}, u32[]{:S(2)}, u32[]{:S(2)}) collective-permute-start(bf16[2,128,512]{2,1,0:T(8,128)(2,1)S(1)} %bitcast.63), channel_id=1, source_target_pairs={{8,0},{12,4},{16,8},{20,12},{24,16},{28,20},{32,24},{36,28},{40,32... | collective-permute-start | bytes 786440 | tf_op jit(solution)/shard_map/ppermute | solution.py:14
  31.6 2.7 %collective-permute-start.2 = (bf16[2,128,512]{2,1,0:T(8,128)(2,1)S(1)}, bf16[2,128,512]{2,1,0:T(8,128)(2,1)S(1)}, u32[]{:S(2)}, u32[]{:S(2)}) collective-permute-start(bf16[2,128,512]{2,1,0:T(8,128)(2,1)S(1)} %bitcast.64), channel_id=1, source_target_pairs={{0,4},{4,8},{8,12},{12,16},{16,20},{20,24},{24,28},{28,32},{32,36}... | collective-permute-start | bytes 786440 | tf_op jit(solution)/shard_map/ppermute | solution.py:14
  34.3 3.6 %collective-permute-start.1 = (bf16[2,128,512]{2,1,0:T(8,128)(2,1)S(1)}, bf16[2,128,512]{2,1,0:T(8,128)(2,1)}, u32[]{:S(2)}, u32[]{:S(2)}) collective-permute-start(bf16[2,128,512]{2,1,0:T(8,128)(2,1)S(1)} %bitcast.65), channel_id=1, source_target_pairs={{0,8},{4,12},{8,16},{12,20},{16,24},{20,28},{24,32},{28,36},{32,40... | collective-permute-start | bytes 786440 | tf_op jit(solution)/shard_map/ppermute | solution.py:14
  38.0 2.3 %collective-permute-start = (bf16[2,128,512]{2,1,0:T(8,128)(2,1)S(1)}, bf16[2,128,512]{2,1,0:T(8,128)(2,1)}, u32[]{:S(2)}, u32[]{:S(2)}) collective-permute-start(bf16[2,128,512]{2,1,0:T(8,128)(2,1)S(1)} %bitcast.66), channel_id=1, source_target_pairs={{0,12},{4,16},{8,20},{12,24},{16,28},{20,32},{24,36},{28,40},{32,4... | collective-permute-start | bytes 786440 | tf_op jit(solution)/shard_map/ppermute | solution.py:14
  40.9 11.3 %collective-permute-done = bf16[2,128,512]{2,1,0:T(8,128)(2,1)} collective-permute-done((bf16[2,128,512]{2,1,0:T(8,128)(2,1)S(1)}, bf16[2,128,512]{2,1,0:T(8,128)(2,1)}, u32[]{:S(2)}, u32[]{:S(2)}) %collective-permute-start) | collective-permute-done | bytes 262176 | tf_op jit(solution)/shard_map/ppermute | solution.py:14
  52.1 1.9 %collective-permute-start.3 = (bf16[2,128,512]{2,1,0:T(8,128)(2,1)S(1)}, bf16[2,128,512]{2,1,0:T(8,128)(2,1)S(1)}, u32[]{:S(2)}, u32[]{:S(2)}) collective-permute-start(bf16[2,128,512]{2,1,0:T(8,128)(2,1)S(1)} %bitcast.67), channel_id=1, source_target_pairs={{4,0},{8,4},{12,8},{16,12},{20,16},{24,20},{28,24},{32,28},{36,32}... | collective-permute-start | bytes 786440 | tf_op jit(solution)/shard_map/ppermute | solution.py:14
  54.1 1.7 constant_dynamic-update-slice_fusion.6
  55.7 1.7 constant_dynamic-update-slice_fusion.5
  61.0 2.2 %gather_fusion = bf16[18,128,512]{2,1,0:T(8,128)(2,1)S(1)} fusion(bf16[14,128,512]{2,1,0:T(8,128)(2,1)} %constant_dynamic-update-slice_fusion, s32[1024]{0:T(1024)S(1)} %pad_clamp_fusion), kind=kCustom, calls=%fused_computation | custom fusion | bytes 4718664 | tf_op jit(solution)/shard_map/gather | solution.py:56
  63.2 2.3 %reshape.43 = bf16[2,1152,2,2,128]{4,3,2,1,0:T(2,128)(2,1)} reshape(bf16[18,128,512]{2,1,0:T(8,128)(2,1)S(1)} %gather_fusion) | data formatting | bytes 4718592 | tf_op jit(solution)/shard_map/reshape | solution.py:56
  65.6 2.9 %fusion.42 = (bf16[2,1152,1,2,128]{4,3,2,1,0:T(2,128)(2,1)S(1)}, bf16[2,1152,1,2,128]{4,3,2,1,0:T(2,128)(2,1)S(1)}) fusion(bf16[2,1152,2,2,128]{4,3,2,1,0:T(2,128)(2,1)} %reshape.43), kind=kLoop, calls=%fused_computation.61 | loop fusion | bytes 4718592 | tf_op jit(solution)/shard_map/slice | solution.py:57
  68.5 2.8 %copy.56 = bf16[2,1152,1,2,128]{1,4,3,0,2:T(8,128)(2,1)} copy(bf16[2,1152,1,2,128]{4,3,2,1,0:T(2,128)(2,1)S(1)} %get-tuple-element.3) | data formatting | bytes 2359296
  75.2 1.6 fusion.16
  76.9 8.9 %copy.48 = f32[2,1152,2,128]{3,2,1,0:T(2,128)S(1)} copy(f32[2,1152,2,128]{3,1,2,0:T(8,128)S(1)} %convolution_bitcast_fusion) | data formatting | bytes 4718592 | tf_op jit(solution)/shard_map/ihqk,iqhd->ikhd/transpose | solution.py:73
  85.8 2.9 %reshape.49 = f32[18,128,256]{2,1,0:T(8,128)} reshape(f32[2,1152,2,128]{3,2,1,0:T(2,128)S(1)} %copy.48) | data formatting | bytes 4718592 | tf_op jit(solution)/shard_map/reshape | solution.py:102
  88.7 3.2 %copy.50 = f32[18,128,256]{2,0,1:T(8,128)S(1)} copy(f32[18,128,256]{2,1,0:T(8,128)} %reshape.49) | data formatting | bytes 4718592 | tf_op jit(solution)/shard_map/reshape | solution.py:102
  91.9 1.9 %fusion.13 = f32[2,1152,2,128]{1,3,2,0:T(8,128)} fusion(bf16[2,128,2,128]{1,3,2,0:T(8,128)(2,1)S(1)} %copy.44, bf16[2,2,128,1152]{3,2,1,0:T(8,128)(2,1)S(1)} %copy-done.4), kind=kOutput, calls=%fused_computation.15 | convolution fusion | flops 151584768 | bytes 3670016 | tf_op jit(solution)/shard_map/ihqk,iqhd->ikhd/dot_general | solution.py:90
  93.8 5.0 %copy.45 = f32[2,1152,2,128]{3,2,1,0:T(2,128)} copy(f32[2,1152,2,128]{1,3,2,0:T(8,128)} %fusion.13) | data formatting | bytes 4718592 | tf_op jit(solution)/shard_map/mul | solution.py:90
  98.7 4.1 %reshape.48 = f32[18,128,256]{2,1,0:T(8,128)} reshape(f32[2,1152,2,128]{3,2,1,0:T(2,128)} %copy.45) | data formatting | bytes 4718592 | tf_op jit(solution)/shard_map/reshape | solution.py:101
  102.9 3.1 %copy.49 = f32[18,128,256]{2,0,1:T(8,128)S(1)} copy(f32[18,128,256]{2,1,0:T(8,128)} %reshape.48) | data formatting | bytes 4718592 | tf_op jit(solution)/shard_map/reshape | solution.py:101
  106.0 3.7 %fusion.1 = bf16[14,128,512]{2,0,1:T(8,128)(2,1)S(1)} fusion(f32[18,128,256]{2,0,1:T(8,128)S(1)} %copy.50, f32[18,128,256]{2,0,1:T(8,128)S(1)} %copy.49, s32[18]{0:T(128)S(1)} %eq.15), kind=kOutput, calls=%fused_computation.2 | convolution fusion | flops 199360768 | bytes 6553672 | tf_op jit(solution)/shard_map/es,sbc->ebc/dot_general | solution.py:106
  112.3 6.3 %collective-permute-start.10 = (bf16[2,128,512]{2,1,0:T(8,128)(2,1)S(1)}, bf16[2,128,512]{2,1,0:T(8,128)(2,1)}, u32[]{:S(2)}, u32[]{:S(2)}) collective-permute-start(bf16[2,128,512]{2,1,0:T(8,128)(2,1)S(1)} %get-tuple-element.6), channel_id=1, source_target_pairs={{0,12},{4,16},{8,20},{12,24},{16,28},{20,32},{24,36},{28,40},{32,4... | collective-permute-start | bytes 786440 | tf_op jit(solution)/shard_map/ppermute | solution.py:14
  118.6 2.6 %collective-permute-start.9 = (bf16[2,128,512]{2,1,0:T(8,128)(2,1)S(1)}, bf16[2,128,512]{2,1,0:T(8,128)(2,1)}, u32[]{:S(2)}, u32[]{:S(2)}) collective-permute-start(bf16[2,128,512]{2,1,0:T(8,128)(2,1)S(1)} %get-tuple-element.7), channel_id=1, source_target_pairs={{8,0},{12,4},{16,8},{20,12},{24,16},{28,20},{32,24},{36,28},{40,32... | collective-permute-start | bytes 786440 | tf_op jit(solution)/shard_map/ppermute | solution.py:14
  121.3 3.2 %collective-permute-start.8 = (bf16[2,128,512]{2,1,0:T(8,128)(2,1)S(1)}, bf16[2,128,512]{2,1,0:T(8,128)(2,1)}, u32[]{:S(2)}, u32[]{:S(2)}) collective-permute-start(bf16[2,128,512]{2,1,0:T(8,128)(2,1)S(1)} %get-tuple-element.8), channel_id=1, source_target_pairs={{0,8},{4,12},{8,16},{12,20},{16,24},{20,28},{24,32},{28,36},{32,40... | collective-permute-start | bytes 786440 | tf_op jit(solution)/shard_map/ppermute | solution.py:14
  124.5 3.0 %collective-permute-start.7 = (bf16[2,128,512]{2,1,0:T(8,128)(2,1)S(1)}, bf16[2,128,512]{2,1,0:T(8,128)(2,1)}, u32[]{:S(2)}, u32[]{:S(2)}) collective-permute-start(bf16[2,128,512]{2,1,0:T(8,128)(2,1)S(1)} %get-tuple-element.9), channel_id=1, source_target_pairs={{4,0},{8,4},{12,8},{16,12},{20,16},{24,20},{28,24},{32,28},{36,32}... | collective-permute-start | bytes 786440 | tf_op jit(solution)/shard_map/ppermute | solution.py:14
  127.5 2.1 %collective-permute-start.6 = (bf16[2,128,512]{2,1,0:T(8,128)(2,1)S(1)}, bf16[2,128,512]{2,1,0:T(8,128)(2,1)}, u32[]{:S(2)}, u32[]{:S(2)}) collective-permute-start(bf16[2,128,512]{2,1,0:T(8,128)(2,1)S(1)} %get-tuple-element.10), channel_id=1, source_target_pairs={{0,4},{4,8},{8,12},{12,16},{16,20},{20,24},{24,28},{28,32},{32,36}... | collective-permute-start | bytes 786440 | tf_op jit(solution)/shard_map/ppermute | solution.py:14
  132.1 2.8 %collective-permute-done.8 = bf16[2,128,512]{2,1,0:T(8,128)(2,1)} collective-permute-done((bf16[2,128,512]{2,1,0:T(8,128)(2,1)S(1)}, bf16[2,128,512]{2,1,0:T(8,128)(2,1)}, u32[]{:S(2)}, u32[]{:S(2)}) %collective-permute-start.8) | collective-permute-done | bytes 262176 | tf_op jit(solution)/shard_map/ppermute | solution.py:14
  134.9 2.4 %collective-permute-done.6 = bf16[2,128,512]{2,1,0:T(8,128)(2,1)} collective-permute-done((bf16[2,128,512]{2,1,0:T(8,128)(2,1)S(1)}, bf16[2,128,512]{2,1,0:T(8,128)(2,1)}, u32[]{:S(2)}, u32[]{:S(2)}) %collective-permute-start.6) | collective-permute-done | bytes 262176 | tf_op jit(solution)/shard_map/ppermute | solution.py:14
  137.3 1.5 add_convert_fusion
  141.1 35.3 %reduce-scatter.2.cloned.1.call-done = bf16[256,256]{1,0:T(8,128)(2,1)} async-done(((bf16[256,1024]{1,0:T(8,128)(2,1)}), bf16[256,256]{1,0:T(8,128)(2,1)}) %reduce-scatter.2.cloned.1.call-update) | async-done | bytes 131088 | tf_op jit(solution)/shard_map/reduce_scatter | solution.py:130
  (64 shorter events, 17.3 us)
Async XLA Ops:
  7.2 169.2 %reduce-scatter.2.cloned.1.call-start = ((), (), s32[]{:S(2)}) async-start(), calls=%async_computation.1 | async-start | bytes 655360 | tf_op jit(solution)/shard_map/reduce_scatter | solution.py:130
  22.3 18.3 %copy-start.2 = (bf16[1024,3,256]{0,2,1:T(8,128)(2,1)}, bf16[1024,3,256]{0,2,1:T(8,128)(2,1)S(1)}, u32[]{:S(2)}) copy-start(bf16[1024,3,256]{0,2,1:T(8,128)(2,1)S(1)} %copy.33) | copy-start | bytes 4718596
  22.3 17.9 %copy-start.9 = (s32[2,9]{1,0:T(2,128)S(1)}, s32[2,9]{1,0:T(2,128)}, u32[]{:S(2)}) copy-start(s32[2,9]{1,0:T(2,128)} %param.6) | copy-start | bytes 220
  22.3 18.2 %copy-start.7 = (bf16[256,256]{1,0:T(8,128)(2,1)S(1)}, bf16[256,256]{1,0:T(8,128)(2,1)}, u32[]{:S(2)}) copy-start(bf16[256,256]{1,0:T(8,128)(2,1)} %param.7) | copy-start | bytes 393220
  23.0 37.3 %collective-permute-start.5 = (bf16[2,128,512]{2,1,0:T(8,128)(2,1)S(1)}, bf16[2,128,512]{2,1,0:T(8,128)(2,1)S(1)}, u32[]{:S(2)}, u32[]{:S(2)}) collective-permute-start(bf16[2,128,512]{2,1,0:T(8,128)(2,1)S(1)} %bitcast.62), channel_id=1, source_target_pairs={{12,0},{16,4},{20,8},{24,12},{28,16},{32,20},{36,24},{40,28},{44,3... | collective-permute-start | bytes 786440 | tf_op jit(solution)/shard_map/ppermute | solution.py:14
  24.3 35.3 %collective-permute-start.4 = (bf16[2,128,512]{2,1,0:T(8,128)(2,1)S(1)}, bf16[2,128,512]{2,1,0:T(8,128)(2,1)S(1)}, u32[]{:S(2)}, u32[]{:S(2)}) collective-permute-start(bf16[2,128,512]{2,1,0:T(8,128)(2,1)S(1)} %bitcast.63), channel_id=1, source_target_pairs={{8,0},{12,4},{16,8},{20,12},{24,16},{28,20},{32,24},{36,28},{40,32... | collective-permute-start | bytes 786440 | tf_op jit(solution)/shard_map/ppermute | solution.py:14
  31.6 25.8 %collective-permute-start.2 = (bf16[2,128,512]{2,1,0:T(8,128)(2,1)S(1)}, bf16[2,128,512]{2,1,0:T(8,128)(2,1)S(1)}, u32[]{:S(2)}, u32[]{:S(2)}) collective-permute-start(bf16[2,128,512]{2,1,0:T(8,128)(2,1)S(1)} %bitcast.64), channel_id=1, source_target_pairs={{0,4},{4,8},{8,12},{12,16},{16,20},{20,24},{24,28},{28,32},{32,36}... | collective-permute-start | bytes 786440 | tf_op jit(solution)/shard_map/ppermute | solution.py:14
  34.3 21.4 %collective-permute-start.1 = (bf16[2,128,512]{2,1,0:T(8,128)(2,1)S(1)}, bf16[2,128,512]{2,1,0:T(8,128)(2,1)}, u32[]{:S(2)}, u32[]{:S(2)}) collective-permute-start(bf16[2,128,512]{2,1,0:T(8,128)(2,1)S(1)} %bitcast.65), channel_id=1, source_target_pairs={{0,8},{4,12},{8,16},{12,20},{16,24},{20,28},{24,32},{28,36},{32,40... | collective-permute-start | bytes 786440 | tf_op jit(solution)/shard_map/ppermute | solution.py:14
  38.0 14.2 %collective-permute-start = (bf16[2,128,512]{2,1,0:T(8,128)(2,1)S(1)}, bf16[2,128,512]{2,1,0:T(8,128)(2,1)}, u32[]{:S(2)}, u32[]{:S(2)}) collective-permute-start(bf16[2,128,512]{2,1,0:T(8,128)(2,1)S(1)} %bitcast.66), channel_id=1, source_target_pairs={{0,12},{4,16},{8,20},{12,24},{16,28},{20,32},{24,36},{28,40},{32,4... | collective-permute-start | bytes 786440 | tf_op jit(solution)/shard_map/ppermute | solution.py:14
  52.1 6.7 %collective-permute-start.3 = (bf16[2,128,512]{2,1,0:T(8,128)(2,1)S(1)}, bf16[2,128,512]{2,1,0:T(8,128)(2,1)S(1)}, u32[]{:S(2)}, u32[]{:S(2)}) collective-permute-start(bf16[2,128,512]{2,1,0:T(8,128)(2,1)S(1)} %bitcast.67), channel_id=1, source_target_pairs={{4,0},{8,4},{12,8},{16,12},{20,16},{24,20},{28,24},{32,28},{36,32}... | collective-permute-start | bytes 786440 | tf_op jit(solution)/shard_map/ppermute | solution.py:14
  68.5 3.4 %copy-start = (bf16[2,1152,1,2,128]{4,3,2,1,0:T(2,128)(2,1)}, bf16[2,1152,1,2,128]{4,3,2,1,0:T(2,128)(2,1)S(1)}, u32[]{:S(2)}) copy-start(bf16[2,1152,1,2,128]{4,3,2,1,0:T(2,128)(2,1)S(1)} %get-tuple-element.2) | copy-start | bytes 3538948
  72.7 1.3 copy-start.6
  88.7 3.2 %copy-start.4 = (bf16[2,2,128,1152]{3,2,1,0:T(8,128)(2,1)S(1)}, bf16[2,2,128,1152]{3,2,1,0:T(8,128)(2,1)}, u32[]{:S(2)}) copy-start(bf16[2,2,128,1152]{3,2,1,0:T(8,128)(2,1)} %fusion.16) | copy-start | bytes 3538948
  110.7 18.9 %copy-start.1 = (bf16[2,1152,1,2,128]{4,3,2,1,0:T(2,128)(2,1)S(1)}, bf16[2,1152,1,2,128]{4,3,2,1,0:T(2,128)(2,1)}, u32[]{:S(2)}) copy-start(bf16[2,1152,1,2,128]{4,3,2,1,0:T(2,128)(2,1)} %copy-done) | copy-start | bytes 3538948
  110.7 18.9 %copy-start.5 = (bf16[2,2,128,1152]{3,2,1,0:T(8,128)(2,1)S(1)}, bf16[2,2,128,1152]{3,2,1,0:T(8,128)(2,1)}, u32[]{:S(2)}) copy-start(bf16[2,2,128,1152]{3,2,1,0:T(8,128)(2,1)} %fusion.16) | copy-start | bytes 3538948
  110.9 16.6 %collective-permute-start.11 = (bf16[2,128,512]{2,1,0:T(8,128)(2,1)S(1)}, bf16[2,128,512]{2,1,0:T(8,128)(2,1)S(1)}, u32[]{:S(2)}, u32[]{:S(2)}) collective-permute-start(bf16[2,128,512]{2,1,0:T(8,128)(2,1)S(1)} %get-tuple-element.5), channel_id=1, source_target_pairs={{12,0},{16,4},{20,8},{24,12},{28,16},{32,20},{36,24},{40,28},{44,3... | collective-permute-start | bytes 786440 | tf_op jit(solution)/shard_map/ppermute | solution.py:14
  112.3 19.7 %collective-permute-start.10 = (bf16[2,128,512]{2,1,0:T(8,128)(2,1)S(1)}, bf16[2,128,512]{2,1,0:T(8,128)(2,1)}, u32[]{:S(2)}, u32[]{:S(2)}) collective-permute-start(bf16[2,128,512]{2,1,0:T(8,128)(2,1)S(1)} %get-tuple-element.6), channel_id=1, source_target_pairs={{0,12},{4,16},{8,20},{12,24},{16,28},{20,32},{24,36},{28,40},{32,4... | collective-permute-start | bytes 786440 | tf_op jit(solution)/shard_map/ppermute | solution.py:14
  118.6 13.4 %collective-permute-start.9 = (bf16[2,128,512]{2,1,0:T(8,128)(2,1)S(1)}, bf16[2,128,512]{2,1,0:T(8,128)(2,1)}, u32[]{:S(2)}, u32[]{:S(2)}) collective-permute-start(bf16[2,128,512]{2,1,0:T(8,128)(2,1)S(1)} %get-tuple-element.7), channel_id=1, source_target_pairs={{8,0},{12,4},{16,8},{20,12},{24,16},{28,20},{32,24},{36,28},{40,32... | collective-permute-start | bytes 786440 | tf_op jit(solution)/shard_map/ppermute | solution.py:14
  121.3 13.6 %collective-permute-start.8 = (bf16[2,128,512]{2,1,0:T(8,128)(2,1)S(1)}, bf16[2,128,512]{2,1,0:T(8,128)(2,1)}, u32[]{:S(2)}, u32[]{:S(2)}) collective-permute-start(bf16[2,128,512]{2,1,0:T(8,128)(2,1)S(1)} %get-tuple-element.8), channel_id=1, source_target_pairs={{0,8},{4,12},{8,16},{12,20},{16,24},{20,28},{24,32},{28,36},{32,40... | collective-permute-start | bytes 786440 | tf_op jit(solution)/shard_map/ppermute | solution.py:14
  124.5 10.4 %collective-permute-start.7 = (bf16[2,128,512]{2,1,0:T(8,128)(2,1)S(1)}, bf16[2,128,512]{2,1,0:T(8,128)(2,1)}, u32[]{:S(2)}, u32[]{:S(2)}) collective-permute-start(bf16[2,128,512]{2,1,0:T(8,128)(2,1)S(1)} %get-tuple-element.9), channel_id=1, source_target_pairs={{4,0},{8,4},{12,8},{16,12},{20,16},{24,20},{28,24},{32,28},{36,32}... | collective-permute-start | bytes 786440 | tf_op jit(solution)/shard_map/ppermute | solution.py:14
  127.5 9.8 %collective-permute-start.6 = (bf16[2,128,512]{2,1,0:T(8,128)(2,1)S(1)}, bf16[2,128,512]{2,1,0:T(8,128)(2,1)}, u32[]{:S(2)}, u32[]{:S(2)}) collective-permute-start(bf16[2,128,512]{2,1,0:T(8,128)(2,1)S(1)} %get-tuple-element.10), channel_id=1, source_target_pairs={{0,4},{4,8},{8,12},{12,16},{16,20},{20,24},{24,28},{28,32},{32,36}... | collective-permute-start | bytes 786440 | tf_op jit(solution)/shard_map/ppermute | solution.py:14
  130.9 8.0 %copy-start.3 = (bf16[1024,3,256]{0,2,1:T(8,128)(2,1)S(1)}, bf16[1024,3,256]{0,2,1:T(8,128)(2,1)}, u32[]{:S(2)}) copy-start(bf16[1024,3,256]{0,2,1:T(8,128)(2,1)} %copy-done.2) | copy-start | bytes 4718596
  138.8 1.4 copy-start.8
Sparse Core Ops, SparseCore 0:
  140.3 36.0 reduce-scatter.1
where the time goes:
time: 184 us; the launch traced here: 183 us
  waiting for transfers between devices  51.9 us (28%)
  local copies, waits for them, and re-layouts  50.5 us (27%)
  starting transfers between devices  37.8 us (21%)
  between operations  14.4 us (8%)
  blocking collectives  13.3 us (7%)
  matrix products  13 us (7%)
  other arithmetic  2.32 us (1%)
    ppermute x12, starting transfers between devices, shifted(): lax.ppermute(value, axis, [(source, source + steps) for source in range(f...  37.7 us
    reduce_scatter x1, waiting for transfers between devices, body(): lax.psum_scatter(partial_sum.astype(jnp.bfloat16), 'head', scatter_dimens...  35.3 us
    ppermute x12, waiting for transfers between devices, shifted(): lax.ppermute(value, axis, [(source, source + steps) for source in range(f...  16.5 us
    all_gather x1, blocking collectives, body(): lax.all_gather(features, 'head', axis=1, tiled=True)  13.3 us
    unnamed x32, local copies, waits for them, and re-layouts  12.1 us
    transpose x1, local copies, waits for them, and re-layouts, body(): jnp.einsum('ihqk,iqhd->ikhd', softmax_share, grad_blocks, preferred_eleme...  8.88 us
    reshape x2, local copies, waits for them, and re-layouts, body(): key_terms.reshape(resident_tiles * slots, BLK, local_width)  7.22 us
    reshape x2, local copies, waits for them, and re-layouts, body(): value_terms.reshape(resident_tiles * slots, BLK, local_width)  6.11 us
  transfers between devices with their start and end apart: 13, of which 4 were waited for; matrix products, arithmetic and copies ran while one was open for 5% of the time, Pallas kernels for 0%

commit v1 on v0

--- a/solution.py
+++ b/solution.py
@@ -6,6 +6,27 @@
 HD = 128
 BLK = 128
 OMAX = 3
+
+
+def gather_around(value, axis, dim):
+    peers, mine, extent = (lax.axis_size(axis), lax.axis_index(axis), value.shape[dim])
+    right = [(i, (i + 1) % peers) for i in range(peers)]
+    left = [(i, (i - 1) % peers) for i in range(peers)]
+    result = jnp.zeros((*value.shape[:dim], peers * extent, *value.shape[dim + 1 :]), value.dtype)
+    result = lax.dynamic_update_slice_in_dim(result, value, mine * extent, axis=dim)
+    from_left = from_right = value
+    half = peers // 2
+    for lap in range(1, half + 1):
+        from_left = lax.ppermute(from_left, axis, right)
+        result = lax.dynamic_update_slice_in_dim(
+            result, from_left, (mine - lap) % peers * extent, axis=dim
+        )
+        if lap < peers - half:
+            from_right = lax.ppermute(from_right, axis, left)
+            result = lax.dynamic_update_slice_in_dim(
+                result, from_right, (mine + lap) % peers * extent, axis=dim
+            )
+    return result
 
 
 def shifted(value, axis, steps):
@@ -27,9 +48,7 @@
     score_scale = HD ** (-0.5)
     w_flat = w_qkv.reshape(model_width, 3 * local_width)
     projected = jnp.dot(
-        lax.all_gather(features, "head", axis=1, tiled=True),
-        w_flat,
-        preferred_element_type=jnp.float32,
+        gather_around(features, "head", 1), w_flat, preferred_element_type=jnp.float32
     )
     projected = projected.astype(jnp.bfloat16)
     query_blocks = projected[:, :local_width].reshape(resident_tiles, BLK, heads_here, HD)

time: 184 us -> 186 us (1.011)
  blocking collectives: 13.3 us -> 0 us
  starting transfers between devices: 37.8 us -> 45.6 us
  waiting for transfers between devices: 51.9 us -> 59 us
    all_gather x1 -> x0, blocking collectives: 13.3 us -> none  [body(): lax.all_gather(features, 'head', axis=1, tiled=True)]
    ppermute x0 -> x3, waiting for transfers between devices: none -> 8.86 us  [the longest x2 8.86 us: gather_around(): from_left = lax.ppermute(from_left, axis, right)]
    ppermute x0 -> x3, starting transfers between devices: none -> 8.5 us  [the longest x1 4.67 us: gather_around(): from_right = lax.ppermute(from_right, axis, left)]
    ppermute x12, waiting for transfers between devices: 16.5 us -> 13.8 us  [shifted(): lax.ppermute(value, axis, [(source, source + steps) for source in range(f...]
    unnamed x32, local copies, waits for them, and re-layouts: 12.1 us -> 10.2 us
  transfers between devices with their start and end apart: 13 -> 16, of which waited for: 4 -> 8; matrix products, arithmetic and copies ran while one was open for 5% -> 6% of each run, Pallas kernels for 0% -> 0%
where the time goes in v1:
time: 186 us; the launch traced here: 185 us
  waiting for transfers between devices  59 us (32%)
  local copies, waits for them, and re-layouts  49.5 us (27%)
  starting transfers between devices  45.6 us (25%)
  between operations  14.6 us (8%)
  matrix products  13.1 us (7%)
  other arithmetic  3 us (2%)
    ppermute x12, starting transfers between devices, shifted(): lax.ppermute(value, axis, [(source, source + steps) for source in range(f...  37 us
    reduce_scatter x1, waiting for transfers between devices, body(): lax.psum_scatter(partial_sum.astype(jnp.bfloat16), 'head', scatter_dimens...  36.3 us
    ppermute x12, waiting for transfers between devices, shifted(): lax.ppermute(value, axis, [(source, source + steps) for source in range(f...  13.8 us
    unnamed x32, local copies, waits for them, and re-layouts  10.2 us
    transpose x1, local copies, waits for them, and re-layouts, body(): jnp.einsum('ihqk,iqhd->ikhd', softmax_share, grad_blocks, preferred_eleme...  8.88 us
    ppermute x2, waiting for transfers between devices, gather_around(): from_left = lax.ppermute(from_left, axis, right)  8.86 us
    reshape x2, local copies, waits for them, and re-layouts, body(): key_terms.reshape(resident_tiles * slots, BLK, local_width)  7.24 us
    reshape x2, local copies, waits for them, and re-layouts, body(): value_terms.reshape(resident_tiles * slots, BLK, local_width)  6.11 us
  transfers between devices with their start and end apart: 16, of which 8 were waited for; matrix products, arithmetic and copies ran while one was open for 6% of the time, Pallas kernels for 0%

profile of v1, /device:TPU:8, one launch (start us, length us, event | category | flops | bytes accessed | tf_op | source)
XLA Modules:
  0.0 184.7 jit_solution(9107496813521246870)
XLA Ops:
  7.2 4.7 %collective-permute-start.1 = (bf16[256,256]{1,0:T(8,128)(2,1)}, bf16[256,256]{1,0:T(8,128)(2,1)S(1)}, u32[]{:S(2)}, u32[]{:S(2)}) collective-permute-start(bf16[256,256]{1,0:T(8,128)(2,1)} %param.4), channel_id=1, source_target_pairs={{0,3},{1,0},{2,1},{3,2},{4,7},{5,4},{6,5},{7,6},{8,11},{9,8},{10,9... | collective-permute-start | bytes 393224 | tf_op jit(solution)/shard_map/ppermute | solution.py:25
  11.9 1.9 %collective-permute-start = (bf16[256,256]{1,0:T(8,128)(2,1)}, bf16[256,256]{1,0:T(8,128)(2,1)S(1)}, u32[]{:S(2)}, u32[]{:S(2)}) collective-permute-start(bf16[256,256]{1,0:T(8,128)(2,1)} %param.4), channel_id=1, source_target_pairs={{0,1},{1,2},{2,3},{3,0},{4,5},{5,6},{6,7},{7,4},{8,9},{9,10},{10,1... | collective-permute-start | bytes 393224 | tf_op jit(solution)/shard_map/ppermute | solution.py:20
  15.6 1.7 copy.33
  17.4 2.8 %collective-permute-done = bf16[256,256]{1,0:T(8,128)(2,1)S(1)} collective-permute-done((bf16[256,256]{1,0:T(8,128)(2,1)}, bf16[256,256]{1,0:T(8,128)(2,1)S(1)}, u32[]{:S(2)}, u32[]{:S(2)}) %collective-permute-start) | collective-permute-done | bytes 131104 | tf_op jit(solution)/shard_map/ppermute | solution.py:20
  20.2 1.9 %collective-permute-start.2 = (bf16[256,256]{1,0:T(8,128)(2,1)S(1)}, bf16[256,256]{1,0:T(8,128)(2,1)S(1)}, u32[]{:S(2)}, u32[]{:S(2)}) collective-permute-start(bf16[256,256]{1,0:T(8,128)(2,1)S(1)} %collective-permute-done), channel_id=1, source_target_pairs={{0,1},{1,2},{2,3},{3,0},{4,5},{5,6},{6,7},{7,4},{8,9},{9,10},{10,1... | collective-permute-start | bytes 393224 | tf_op jit(solution)/shard_map/ppermute | solution.py:20
  22.2 6.1 %collective-permute-done.2 = bf16[256,256]{1,0:T(8,128)(2,1)S(1)} collective-permute-done((bf16[256,256]{1,0:T(8,128)(2,1)S(1)}, bf16[256,256]{1,0:T(8,128)(2,1)S(1)}, u32[]{:S(2)}, u32[]{:S(2)}) %collective-permute-start.2) | collective-permute-done | bytes 131104 | tf_op jit(solution)/shard_map/ppermute | solution.py:20
  28.9 3.5 %collective-permute-start.4 = (bf16[2,128,512]{2,1,0:T(8,128)(2,1)S(1)}, bf16[2,128,512]{2,1,0:T(8,128)(2,1)S(1)}, u32[]{:S(2)}, u32[]{:S(2)}) collective-permute-start(bf16[2,128,512]{2,1,0:T(8,128)(2,1)S(1)} %bitcast.62), channel_id=1, source_target_pairs={{0,8},{4,12},{8,16},{12,20},{16,24},{20,28},{24,32},{28,36},{32,40... | collective-permute-start | bytes 786440 | tf_op jit(solution)/shard_map/ppermute | solution.py:35
  33.8 6.4 %collective-permute-start.5 = (bf16[2,128,512]{2,1,0:T(8,128)(2,1)S(1)}, bf16[2,128,512]{2,1,0:T(8,128)(2,1)S(1)}, u32[]{:S(2)}, u32[]{:S(2)}) collective-permute-start(bf16[2,128,512]{2,1,0:T(8,128)(2,1)S(1)} %bitcast.64), channel_id=1, source_target_pairs={{0,4},{4,8},{8,12},{12,16},{16,20},{20,24},{24,28},{28,32},{32,36}... | collective-permute-start | bytes 786440 | tf_op jit(solution)/shard_map/ppermute | solution.py:35
  41.8 1.9 %collective-permute-start.7 = (bf16[2,128,512]{2,1,0:T(8,128)(2,1)S(1)}, bf16[2,128,512]{2,1,0:T(8,128)(2,1)S(1)}, u32[]{:S(2)}, u32[]{:S(2)}) collective-permute-start(bf16[2,128,512]{2,1,0:T(8,128)(2,1)S(1)} %bitcast.66), channel_id=1, source_target_pairs={{8,0},{12,4},{16,8},{20,12},{24,16},{28,20},{32,24},{36,28},{40,32... | collective-permute-start | bytes 786440 | tf_op jit(solution)/shard_map/ppermute | solution.py:35
  44.0 1.9 %collective-permute-start.6 = (bf16[2,128,512]{2,1,0:T(8,128)(2,1)S(1)}, bf16[2,128,512]{2,1,0:T(8,128)(2,1)S(1)}, u32[]{:S(2)}, u32[]{:S(2)}) collective-permute-start(bf16[2,128,512]{2,1,0:T(8,128)(2,1)S(1)} %bitcast.67), channel_id=1, source_target_pairs={{4,0},{8,4},{12,8},{16,12},{20,16},{24,20},{28,24},{32,28},{36,32}... | collective-permute-start | bytes 786440 | tf_op jit(solution)/shard_map/ppermute | solution.py:35
  50.3 6.6 %collective-permute-done.6 = bf16[2,128,512]{2,1,0:T(8,128)(2,1)S(1)} collective-permute-done((bf16[2,128,512]{2,1,0:T(8,128)(2,1)S(1)}, bf16[2,128,512]{2,1,0:T(8,128)(2,1)S(1)}, u32[]{:S(2)}, u32[]{:S(2)}) %collective-permute-start.6) | collective-permute-done | bytes 262176 | tf_op jit(solution)/shard_map/ppermute | solution.py:35
  59.4 2.2 %gather_fusion = bf16[18,128,512]{2,1,0:T(8,128)(2,1)S(1)} fusion(bf16[14,128,512]{2,1,0:T(8,128)(2,1)} %constant_dynamic-update-slice_fusion, s32[1024]{0:T(1024)S(1)} %pad_clamp_fusion), kind=kCustom, calls=%fused_computation | custom fusion | bytes 4718664 | tf_op jit(solution)/shard_map/gather | solution.py:75
  61.6 2.3 %reshape.43 = bf16[2,1152,2,2,128]{4,3,2,1,0:T(2,128)(2,1)} reshape(bf16[18,128,512]{2,1,0:T(8,128)(2,1)S(1)} %gather_fusion) | data formatting | bytes 4718592 | tf_op jit(solution)/shard_map/reshape | solution.py:75
  63.9 2.9 %fusion.42 = (bf16[2,1152,1,2,128]{4,3,2,1,0:T(2,128)(2,1)S(1)}, bf16[2,1152,1,2,128]{4,3,2,1,0:T(2,128)(2,1)S(1)}) fusion(bf16[2,1152,2,2,128]{4,3,2,1,0:T(2,128)(2,1)} %reshape.43), kind=kLoop, calls=%fused_computation.65 | loop fusion | bytes 4718592 | tf_op jit(solution)/shard_map/slice | solution.py:76
  66.9 2.8 %copy.56 = bf16[2,1152,1,2,128]{1,4,3,0,2:T(8,128)(2,1)} copy(bf16[2,1152,1,2,128]{4,3,2,1,0:T(2,128)(2,1)S(1)} %get-tuple-element.3) | data formatting | bytes 2359296
  73.6 1.6 fusion.16
  75.3 8.9 %copy.48 = f32[2,1152,2,128]{3,2,1,0:T(2,128)S(1)} copy(f32[2,1152,2,128]{3,1,2,0:T(8,128)S(1)} %convolution_bitcast_fusion) | data formatting | bytes 4718592 | tf_op jit(solution)/shard_map/ihqk,iqhd->ikhd/transpose | solution.py:92
  84.2 2.9 %reshape.49 = f32[18,128,256]{2,1,0:T(8,128)} reshape(f32[2,1152,2,128]{3,2,1,0:T(2,128)S(1)} %copy.48) | data formatting | bytes 4718592 | tf_op jit(solution)/shard_map/reshape | solution.py:121
  87.1 3.2 %copy.50 = f32[18,128,256]{2,0,1:T(8,128)S(1)} copy(f32[18,128,256]{2,1,0:T(8,128)} %reshape.49) | data formatting | bytes 4718592 | tf_op jit(solution)/shard_map/reshape | solution.py:121
  90.3 1.9 %fusion.13 = f32[2,1152,2,128]{1,3,2,0:T(8,128)} fusion(bf16[2,128,2,128]{1,3,2,0:T(8,128)(2,1)S(1)} %copy.44, bf16[2,2,128,1152]{3,2,1,0:T(8,128)(2,1)S(1)} %copy-done.4), kind=kOutput, calls=%fused_computation.15 | convolution fusion | flops 151584768 | bytes 3670016 | tf_op jit(solution)/shard_map/ihqk,iqhd->ikhd/dot_general | solution.py:109
  92.2 5.0 %copy.45 = f32[2,1152,2,128]{3,2,1,0:T(2,128)} copy(f32[2,1152,2,128]{1,3,2,0:T(8,128)} %fusion.13) | data formatting | bytes 4718592 | tf_op jit(solution)/shard_map/mul | solution.py:109
  97.1 4.2 %reshape.48 = f32[18,128,256]{2,1,0:T(8,128)} reshape(f32[2,1152,2,128]{3,2,1,0:T(2,128)} %copy.45) | data formatting | bytes 4718592 | tf_op jit(solution)/shard_map/reshape | solution.py:120
  101.3 3.1 %copy.49 = f32[18,128,256]{2,0,1:T(8,128)S(1)} copy(f32[18,128,256]{2,1,0:T(8,128)} %reshape.48) | data formatting | bytes 4718592 | tf_op jit(solution)/shard_map/reshape | solution.py:120
  104.4 3.7 %fusion.1 = bf16[14,128,512]{2,0,1:T(8,128)(2,1)S(1)} fusion(f32[18,128,256]{2,0,1:T(8,128)S(1)} %copy.50, f32[18,128,256]{2,0,1:T(8,128)S(1)} %copy.49, s32[18]{0:T(128)S(1)} %eq.19), kind=kOutput, calls=%fused_computation.2 | convolution fusion | flops 199360768 | bytes 6553672 | tf_op jit(solution)/shard_map/es,sbc->ebc/dot_general | solution.py:125
  110.8 8.4 %collective-permute-start.13 = (bf16[2,128,512]{2,1,0:T(8,128)(2,1)S(1)}, bf16[2,128,512]{2,1,0:T(8,128)(2,1)}, u32[]{:S(2)}, u32[]{:S(2)}) collective-permute-start(bf16[2,128,512]{2,1,0:T(8,128)(2,1)S(1)} %get-tuple-element.6), channel_id=1, source_target_pairs={{0,12},{4,16},{8,20},{12,24},{16,28},{20,32},{24,36},{28,40},{32,4... | collective-permute-start | bytes 786440 | tf_op jit(solution)/shard_map/ppermute | solution.py:35
  119.1 2.5 %collective-permute-start.12 = (bf16[2,128,512]{2,1,0:T(8,128)(2,1)S(1)}, bf16[2,128,512]{2,1,0:T(8,128)(2,1)}, u32[]{:S(2)}, u32[]{:S(2)}) collective-permute-start(bf16[2,128,512]{2,1,0:T(8,128)(2,1)S(1)} %get-tuple-element.7), channel_id=1, source_target_pairs={{8,0},{12,4},{16,8},{20,12},{24,16},{28,20},{32,24},{36,28},{40,32... | collective-permute-start | bytes 786440 | tf_op jit(solution)/shard_map/ppermute | solution.py:35
  121.6 3.3 %collective-permute-start.11 = (bf16[2,128,512]{2,1,0:T(8,128)(2,1)S(1)}, bf16[2,128,512]{2,1,0:T(8,128)(2,1)}, u32[]{:S(2)}, u32[]{:S(2)}) collective-permute-start(bf16[2,128,512]{2,1,0:T(8,128)(2,1)S(1)} %get-tuple-element.8), channel_id=1, source_target_pairs={{0,8},{4,12},{8,16},{12,20},{16,24},{20,28},{24,32},{28,36},{32,40... | collective-permute-start | bytes 786440 | tf_op jit(solution)/shard_map/ppermute | solution.py:35
  125.0 2.8 %collective-permute-start.10 = (bf16[2,128,512]{2,1,0:T(8,128)(2,1)S(1)}, bf16[2,128,512]{2,1,0:T(8,128)(2,1)}, u32[]{:S(2)}, u32[]{:S(2)}) collective-permute-start(bf16[2,128,512]{2,1,0:T(8,128)(2,1)S(1)} %get-tuple-element.9), channel_id=1, source_target_pairs={{4,0},{8,4},{12,8},{16,12},{20,16},{24,20},{28,24},{32,28},{36,32}... | collective-permute-start | bytes 786440 | tf_op jit(solution)/shard_map/ppermute | solution.py:35
  127.8 2.2 %collective-permute-start.9 = (bf16[2,128,512]{2,1,0:T(8,128)(2,1)S(1)}, bf16[2,128,512]{2,1,0:T(8,128)(2,1)}, u32[]{:S(2)}, u32[]{:S(2)}) collective-permute-start(bf16[2,128,512]{2,1,0:T(8,128)(2,1)S(1)} %get-tuple-element.10), channel_id=1, source_target_pairs={{0,4},{4,8},{8,12},{12,16},{16,20},{20,24},{24,28},{28,32},{32,36}... | collective-permute-start | bytes 786440 | tf_op jit(solution)/shard_map/ppermute | solution.py:35
  132.6 3.0 %collective-permute-done.11 = bf16[2,128,512]{2,1,0:T(8,128)(2,1)} collective-permute-done((bf16[2,128,512]{2,1,0:T(8,128)(2,1)S(1)}, bf16[2,128,512]{2,1,0:T(8,128)(2,1)}, u32[]{:S(2)}, u32[]{:S(2)}) %collective-permute-start.11) | collective-permute-done | bytes 262176 | tf_op jit(solution)/shard_map/ppermute | solution.py:35
  135.5 2.2 %collective-permute-done.9 = bf16[2,128,512]{2,1,0:T(8,128)(2,1)} collective-permute-done((bf16[2,128,512]{2,1,0:T(8,128)(2,1)S(1)}, bf16[2,128,512]{2,1,0:T(8,128)(2,1)}, u32[]{:S(2)}, u32[]{:S(2)}) %collective-permute-start.9) | collective-permute-done | bytes 262176 | tf_op jit(solution)/shard_map/ppermute | solution.py:35
  141.5 36.3 %reduce-scatter.2.cloned.1.call-done = bf16[256,256]{1,0:T(8,128)(2,1)} async-done(((bf16[256,1024]{1,0:T(8,128)(2,1)}), bf16[256,256]{1,0:T(8,128)(2,1)}) %reduce-scatter.2.cloned.1.call-update) | async-done | bytes 131088 | tf_op jit(solution)/shard_map/reduce_scatter | solution.py:149
  (74 shorter events, 25.2 us)
Async XLA Ops:
  7.2 170.7 %reduce-scatter.2.cloned.1.call-start = ((), (), s32[]{:S(2)}) async-start(), calls=%async_computation.1 | async-start | bytes 655360 | tf_op jit(solution)/shard_map/reduce_scatter | solution.py:149
  7.2 14.9 %collective-permute-start.1 = (bf16[256,256]{1,0:T(8,128)(2,1)}, bf16[256,256]{1,0:T(8,128)(2,1)S(1)}, u32[]{:S(2)}, u32[]{:S(2)}) collective-permute-start(bf16[256,256]{1,0:T(8,128)(2,1)} %param.4), channel_id=1, source_target_pairs={{0,3},{1,0},{2,1},{3,2},{4,7},{5,4},{6,5},{7,6},{8,11},{9,8},{10,9... | collective-permute-start | bytes 393224 | tf_op jit(solution)/shard_map/ppermute | solution.py:25
  11.9 8.3 %collective-permute-start = (bf16[256,256]{1,0:T(8,128)(2,1)}, bf16[256,256]{1,0:T(8,128)(2,1)S(1)}, u32[]{:S(2)}, u32[]{:S(2)}) collective-permute-start(bf16[256,256]{1,0:T(8,128)(2,1)} %param.4), channel_id=1, source_target_pairs={{0,1},{1,2},{2,3},{3,0},{4,5},{5,6},{6,7},{7,4},{8,9},{9,10},{10,1... | collective-permute-start | bytes 393224 | tf_op jit(solution)/shard_map/ppermute | solution.py:20
  17.3 11.6 %copy-start.2 = (bf16[1024,3,256]{0,2,1:T(8,128)(2,1)}, bf16[1024,3,256]{0,2,1:T(8,128)(2,1)S(1)}, u32[]{:S(2)}) copy-start(bf16[1024,3,256]{0,2,1:T(8,128)(2,1)S(1)} %copy.33) | copy-start | bytes 4718596
  20.2 8.1 %collective-permute-start.2 = (bf16[256,256]{1,0:T(8,128)(2,1)S(1)}, bf16[256,256]{1,0:T(8,128)(2,1)S(1)}, u32[]{:S(2)}, u32[]{:S(2)}) collective-permute-start(bf16[256,256]{1,0:T(8,128)(2,1)S(1)} %collective-permute-done), channel_id=1, source_target_pairs={{0,1},{1,2},{2,3},{3,0},{4,5},{5,6},{6,7},{7,4},{8,9},{9,10},{10,1... | collective-permute-start | bytes 393224 | tf_op jit(solution)/shard_map/ppermute | solution.py:20
  22.1 11.6 %copy-start.9 = (s32[2,9]{1,0:T(2,128)S(1)}, s32[2,9]{1,0:T(2,128)}, u32[]{:S(2)}) copy-start(s32[2,9]{1,0:T(2,128)} %param.6) | copy-start | bytes 220
  22.1 18.2 %copy-start.7 = (bf16[256,256]{1,0:T(8,128)(2,1)S(1)}, bf16[256,256]{1,0:T(8,128)(2,1)}, u32[]{:S(2)}) copy-start(bf16[256,256]{1,0:T(8,128)(2,1)} %param.7) | copy-start | bytes 393220
  28.9 17.7 %collective-permute-start.4 = (bf16[2,128,512]{2,1,0:T(8,128)(2,1)S(1)}, bf16[2,128,512]{2,1,0:T(8,128)(2,1)S(1)}, u32[]{:S(2)}, u32[]{:S(2)}) collective-permute-start(bf16[2,128,512]{2,1,0:T(8,128)(2,1)S(1)} %bitcast.62), channel_id=1, source_target_pairs={{0,8},{4,12},{8,16},{12,20},{16,24},{20,28},{24,32},{28,36},{32,40... | collective-permute-start | bytes 786440 | tf_op jit(solution)/shard_map/ppermute | solution.py:35
  32.4 11.5 %collective-permute-start.3 = (bf16[2,128,512]{2,1,0:T(8,128)(2,1)S(1)}, bf16[2,128,512]{2,1,0:T(8,128)(2,1)S(1)}, u32[]{:S(2)}, u32[]{:S(2)}) collective-permute-start(bf16[2,128,512]{2,1,0:T(8,128)(2,1)S(1)} %bitcast.63), channel_id=1, source_target_pairs={{0,12},{4,16},{8,20},{12,24},{16,28},{20,32},{24,36},{28,40},{32,4... | collective-permute-start | bytes 786440 | tf_op jit(solution)/shard_map/ppermute | solution.py:35
  33.8 15.0 %collective-permute-start.5 = (bf16[2,128,512]{2,1,0:T(8,128)(2,1)S(1)}, bf16[2,128,512]{2,1,0:T(8,128)(2,1)S(1)}, u32[]{:S(2)}, u32[]{:S(2)}) collective-permute-start(bf16[2,128,512]{2,1,0:T(8,128)(2,1)S(1)} %bitcast.64), channel_id=1, source_target_pairs={{0,4},{4,8},{8,12},{12,16},{16,20},{20,24},{24,28},{28,32},{32,36}... | collective-permute-start | bytes 786440 | tf_op jit(solution)/shard_map/ppermute | solution.py:35
  40.5 18.2 %collective-permute-start.8 = (bf16[2,128,512]{2,1,0:T(8,128)(2,1)S(1)}, bf16[2,128,512]{2,1,0:T(8,128)(2,1)S(1)}, u32[]{:S(2)}, u32[]{:S(2)}) collective-permute-start(bf16[2,128,512]{2,1,0:T(8,128)(2,1)S(1)} %bitcast.65), channel_id=1, source_target_pairs={{12,0},{16,4},{20,8},{24,12},{28,16},{32,20},{36,24},{40,28},{44,3... | collective-permute-start | bytes 786440 | tf_op jit(solution)/shard_map/ppermute | solution.py:35
  41.8 16.1 %collective-permute-start.7 = (bf16[2,128,512]{2,1,0:T(8,128)(2,1)S(1)}, bf16[2,128,512]{2,1,0:T(8,128)(2,1)S(1)}, u32[]{:S(2)}, u32[]{:S(2)}) collective-permute-start(bf16[2,128,512]{2,1,0:T(8,128)(2,1)S(1)} %bitcast.66), channel_id=1, source_target_pairs={{8,0},{12,4},{16,8},{20,12},{24,16},{28,20},{32,24},{36,28},{40,32... | collective-permute-start | bytes 786440 | tf_op jit(solution)/shard_map/ppermute | solution.py:35
  44.0 12.9 %collective-permute-start.6 = (bf16[2,128,512]{2,1,0:T(8,128)(2,1)S(1)}, bf16[2,128,512]{2,1,0:T(8,128)(2,1)S(1)}, u32[]{:S(2)}, u32[]{:S(2)}) collective-permute-start(bf16[2,128,512]{2,1,0:T(8,128)(2,1)S(1)} %bitcast.67), channel_id=1, source_target_pairs={{4,0},{8,4},{12,8},{16,12},{20,16},{24,20},{28,24},{32,28},{36,32}... | collective-permute-start | bytes 786440 | tf_op jit(solution)/shard_map/ppermute | solution.py:35
  66.9 3.4 %copy-start = (bf16[2,1152,1,2,128]{4,3,2,1,0:T(2,128)(2,1)}, bf16[2,1152,1,2,128]{4,3,2,1,0:T(2,128)(2,1)S(1)}, u32[]{:S(2)}) copy-start(bf16[2,1152,1,2,128]{4,3,2,1,0:T(2,128)(2,1)S(1)} %get-tuple-element.2) | copy-start | bytes 3538948
  71.1 1.3 copy-start.6
  87.1 3.2 %copy-start.4 = (bf16[2,2,128,1152]{3,2,1,0:T(8,128)(2,1)S(1)}, bf16[2,2,128,1152]{3,2,1,0:T(8,128)(2,1)}, u32[]{:S(2)}) copy-start(bf16[2,2,128,1152]{3,2,1,0:T(8,128)(2,1)} %fusion.16) | copy-start | bytes 3538948
  109.1 21.0 %copy-start.1 = (bf16[2,1152,1,2,128]{4,3,2,1,0:T(2,128)(2,1)S(1)}, bf16[2,1152,1,2,128]{4,3,2,1,0:T(2,128)(2,1)}, u32[]{:S(2)}) copy-start(bf16[2,1152,1,2,128]{4,3,2,1,0:T(2,128)(2,1)} %copy-done) | copy-start | bytes 3538948
  109.1 21.0 %copy-start.5 = (bf16[2,2,128,1152]{3,2,1,0:T(8,128)(2,1)S(1)}, bf16[2,2,128,1152]{3,2,1,0:T(8,128)(2,1)}, u32[]{:S(2)}) copy-start(bf16[2,2,128,1152]{3,2,1,0:T(8,128)(2,1)} %fusion.16) | copy-start | bytes 3538948
  109.3 18.5 %collective-permute-start.14 = (bf16[2,128,512]{2,1,0:T(8,128)(2,1)S(1)}, bf16[2,128,512]{2,1,0:T(8,128)(2,1)S(1)}, u32[]{:S(2)}, u32[]{:S(2)}) collective-permute-start(bf16[2,128,512]{2,1,0:T(8,128)(2,1)S(1)} %get-tuple-element.5), channel_id=1, source_target_pairs={{12,0},{16,4},{20,8},{24,12},{28,16},{32,20},{36,24},{40,28},{44,3... | collective-permute-start | bytes 786440 | tf_op jit(solution)/shard_map/ppermute | solution.py:35
  110.8 21.8 %collective-permute-start.13 = (bf16[2,128,512]{2,1,0:T(8,128)(2,1)S(1)}, bf16[2,128,512]{2,1,0:T(8,128)(2,1)}, u32[]{:S(2)}, u32[]{:S(2)}) collective-permute-start(bf16[2,128,512]{2,1,0:T(8,128)(2,1)S(1)} %get-tuple-element.6), channel_id=1, source_target_pairs={{0,12},{4,16},{8,20},{12,24},{16,28},{20,32},{24,36},{28,40},{32,4... | collective-permute-start | bytes 786440 | tf_op jit(solution)/shard_map/ppermute | solution.py:35
  119.1 13.4 %collective-permute-start.12 = (bf16[2,128,512]{2,1,0:T(8,128)(2,1)S(1)}, bf16[2,128,512]{2,1,0:T(8,128)(2,1)}, u32[]{:S(2)}, u32[]{:S(2)}) collective-permute-start(bf16[2,128,512]{2,1,0:T(8,128)(2,1)S(1)} %get-tuple-element.7), channel_id=1, source_target_pairs={{8,0},{12,4},{16,8},{20,12},{24,16},{28,20},{32,24},{36,28},{40,32... | collective-permute-start | bytes 786440 | tf_op jit(solution)/shard_map/ppermute | solution.py:35
  121.6 13.9 %collective-permute-start.11 = (bf16[2,128,512]{2,1,0:T(8,128)(2,1)S(1)}, bf16[2,128,512]{2,1,0:T(8,128)(2,1)}, u32[]{:S(2)}, u32[]{:S(2)}) collective-permute-start(bf16[2,128,512]{2,1,0:T(8,128)(2,1)S(1)} %get-tuple-element.8), channel_id=1, source_target_pairs={{0,8},{4,12},{8,16},{12,20},{16,24},{20,28},{24,32},{28,36},{32,40... | collective-permute-start | bytes 786440 | tf_op jit(solution)/shard_map/ppermute | solution.py:35
  125.0 10.6 %collective-permute-start.10 = (bf16[2,128,512]{2,1,0:T(8,128)(2,1)S(1)}, bf16[2,128,512]{2,1,0:T(8,128)(2,1)}, u32[]{:S(2)}, u32[]{:S(2)}) collective-permute-start(bf16[2,128,512]{2,1,0:T(8,128)(2,1)S(1)} %get-tuple-element.9), channel_id=1, source_target_pairs={{4,0},{8,4},{12,8},{16,12},{20,16},{24,20},{28,24},{32,28},{36,32}... | collective-permute-start | bytes 786440 | tf_op jit(solution)/shard_map/ppermute | solution.py:35
  127.8 9.9 %collective-permute-start.9 = (bf16[2,128,512]{2,1,0:T(8,128)(2,1)S(1)}, bf16[2,128,512]{2,1,0:T(8,128)(2,1)}, u32[]{:S(2)}, u32[]{:S(2)}) collective-permute-start(bf16[2,128,512]{2,1,0:T(8,128)(2,1)S(1)} %get-tuple-element.10), channel_id=1, source_target_pairs={{0,4},{4,8},{8,12},{12,16},{16,20},{20,24},{24,28},{28,32},{32,36}... | collective-permute-start | bytes 786440 | tf_op jit(solution)/shard_map/ppermute | solution.py:35
  131.4 7.9 %copy-start.3 = (bf16[1024,3,256]{0,2,1:T(8,128)(2,1)S(1)}, bf16[1024,3,256]{0,2,1:T(8,128)(2,1)}, u32[]{:S(2)}) copy-start(bf16[1024,3,256]{0,2,1:T(8,128)(2,1)} %copy-done.2) | copy-start | bytes 4718596
  139.3 1.4 copy-start.8
Sparse Core Ops, SparseCore 0:
  140.8 36.9 reduce-scatter.1
